TPU v7x, 32 devices: a whole 2x2x4 slice. The times are simulated.
32 devices in a mesh: src: 8 (over z, x), att: 4 (over y, core).
Axes of the slice: x: 2, y: 2, z: 4, core: 2. Of those that a mesh axis runs over, the one named last changes fastest.
Arguments:
- residual: float32 [262144], P(('src', 'att')), may hold values from -6 to 6
- weight: float32 [262144], P(('src', 'att')), may hold values from 0.2 to 5
- source_part: float32 [5, 262144], P(None, ('src', 'att')), may hold values from -6 to 6
- attitude_part: float32 [4, 262144], P(None, ('src', 'att')), may hold values from -6 to 6
- calib_part: float32 [262144], P(('src', 'att')), may hold values from -6 to 6
- phase: float32 [262144], P(('src', 'att')), may hold values from 0 to 1
- obs_source: int32 [262144], P(('src', 'att')), may hold values from 0 to 63
- obs_owner: int32 [262144], P(('src', 'att')), may hold values from 0 to 31
- obs_slot: int32 [262144], P(('src', 'att')), may hold values from 0 to 3
- obs_knot: int32 [262144], P(('src', 'att')), may hold values from 0 to 124
- obs_calib: int32 [262144], P(('src', 'att')), may hold values from 0 to 2047
- tile_count: int32 [32, 4], P(('src', 'att')), may hold values from 1 to 2048, 5120 in all within a row
- time_list: int32 [32, 32, 4], P(None, ('src', 'att')), may hold values from 0 to 7
Outputs:
- source_update: float32 [5, 8192], P(None, ('src', 'att'))
- attitude_update: float32 [4, 32768], P(None, ('src', 'att'))
- calib_update: float32 [2048], replicated
- residual_out: float32 [262144], P(('src', 'att'))
Inputs may be any that keep to these rules, and one draw needn't show every extreme that they name: `tile_count`: each device's tile counts sum to 5120. `time_list`: local knot block of the owner; entries may repeat.
All inputs are finite; a program needn't handle non-finite values.
Results may differ from a plain program's by a relative error of at most 0.0001.
Values sent between devices are 32-bit elements; how exact they have to be, the bound alone decides.
A program may use at most 64 MiB of HBM per device.

v0:
```python
import math
import jax
import jax.numpy as jnp
from jax import lax
from jax.sharding import PartitionSpec as P

OBS_TILE = 2048
SRC_TILE = 64
KNOT = 128
LIST = 4
KB_DEV = 8
NCAL = 2048
HIGH = lax.Precision.HIGHEST


def spline_weights(phase):
    other = 1.0 - phase
    square = phase * phase
    cube = square * phase
    return [
        other * other * other / 6.0,
        (3.0 * cube - 6.0 * square + 4.0) / 6.0,
        (-3.0 * cube + 3.0 * square + 3.0 * phase + 1.0) / 6.0,
        cube / 6.0,
    ]


def solve_normals(sums):
    matrix = [[None] * 5 for _ in range(5)]
    column = 0
    for left in range(5):
        for right in range(left, 5):
            matrix[left][right] = sums[:, column]
            matrix[right][left] = sums[:, column]
            column += 1
    target = [sums[:, 15 + left] for left in range(5)]
    for left in range(5):
        matrix[left][left] = matrix[left][left] + 1.0
    for pivot in range(5):
        for lower in range(pivot + 1, 5):
            factor = matrix[lower][pivot] / matrix[pivot][pivot]
            for right in range(pivot, 5):
                matrix[lower][right] = matrix[lower][right] - factor * matrix[pivot][right]
            target[lower] = target[lower] - factor * target[pivot]
    result = [None] * 5
    for pivot in range(4, -1, -1):
        value = target[pivot]
        for right in range(pivot + 1, 5):
            value = value - matrix[pivot][right] * result[right]
        result[pivot] = value / matrix[pivot][pivot]
    return jnp.stack(result, 0)


def knot_rows(basis_rows, knot_first, squared):
    knots = knot_first.shape[0]
    positions = jnp.arange(KNOT, dtype=jnp.int32)[None, :]
    total = jnp.zeros((knots, KNOT), jnp.float32)
    for offset in range(4):
        value = basis_rows[:, offset]
        if squared:
            value = value * value
        total = total + jnp.where(
            positions == knot_first[:, None] + offset, value[:, None], jnp.float32(0.0)
        )
    return total


def on_device(
    residual,
    weight,
    source_part,
    attitude_part,
    calib_part,
    phase,
    obs_source,
    obs_owner,
    obs_slot,
    obs_knot,
    obs_calib,
    tile_count,
    time_list,
):
    count = residual.shape[0]
    devices = lax.axis_size(("src", "att"))
    tiles = tile_count.shape[1]
    index = jnp.arange(count, dtype=jnp.int32)
    live = (index % OBS_TILE).reshape(tiles, OBS_TILE) < tile_count.reshape(tiles, 1)
    weighted = jnp.where(live.reshape(count), weight, jnp.float32(0.0))
    onehot = (
        obs_source.reshape(tiles, OBS_TILE)[:, :, None]
        == jnp.arange(SRC_TILE, dtype=jnp.int32)[None, None, :]
    ).astype(jnp.float32)
    columns = []
    for left in range(5):
        for right in range(left, 5):
            columns.append(weighted * source_part[left] * source_part[right])
    for left in range(5):
        columns.append(weighted * source_part[left] * residual)
    stacked = jnp.stack(columns, 0).reshape(20, tiles, OBS_TILE)
    sums = jnp.einsum(
        "tos,cto->tsc", onehot, stacked, precision=HIGH, preferred_element_type=jnp.float32
    )
    source_update = solve_normals(sums.reshape(tiles * SRC_TILE, 20))
    per_obs = jnp.einsum(
        "tos,kts->kto",
        onehot,
        source_update.reshape(5, tiles, SRC_TILE),
        precision=HIGH,
        preferred_element_type=jnp.float32,
    )
    first = residual - jnp.sum(source_part * per_obs.reshape(5, count), axis=0)
    basis_rows = jnp.stack(spline_weights(phase), 1)
    attitude_rows = attitude_part.T
    listed_blocks = devices * LIST
    block_id = obs_owner * LIST + obs_slot
    rhs_terms = weighted[:, None] * attitude_rows * first[:, None]
    diag_terms = weighted[:, None] * attitude_rows * attitude_rows
    calib_terms_obs = jnp.stack(
        [weighted * calib_part * first, weighted * calib_part * calib_part], 1
    )
    step_rows = math.gcd(count, 2048)
    steps = count // step_rows
    block_ids = jnp.arange(listed_blocks, dtype=jnp.int32)[None, :]
    calib_ids = jnp.arange(NCAL, dtype=jnp.int32)[None, :]

    def accumulate(carry, inputs):
        partial_value, calib_sum = carry
        blocks, knot_first, basis_part, rhs_part, diag_part, calib_ids_part, calib_vals = inputs
        linear = knot_rows(basis_part, knot_first, False)
        squares = knot_rows(basis_part, knot_first, True)
        spread = jnp.concatenate(
            [
                linear[:, :, None] * rhs_part[:, None, :],
                squares[:, :, None] * diag_part[:, None, :],
            ],
            axis=2,
        )
        spread = spread.reshape(step_rows, KNOT * 8)
        selector = (blocks[:, None] == block_ids).astype(jnp.float32)
        partial_value = partial_value + jnp.einsum(
            "ib,im->bm", selector, spread, precision=HIGH, preferred_element_type=jnp.float32
        )
        calib_hot = (calib_ids_part[:, None] == calib_ids).astype(jnp.float32)
        calib_sum = calib_sum + jnp.einsum(
            "in,ic->cn", calib_hot, calib_vals, precision=HIGH, preferred_element_type=jnp.float32
        )
        return ((partial_value, calib_sum), None)

    inputs = (
        block_id.reshape(steps, step_rows),
        obs_knot.reshape(steps, step_rows),
        basis_rows.reshape(steps, step_rows, 4),
        rhs_terms.reshape(steps, step_rows, 4),
        diag_terms.reshape(steps, step_rows, 4),
        obs_calib.reshape(steps, step_rows),
        calib_terms_obs.reshape(steps, step_rows, 2),
    )
    start = (jnp.zeros((listed_blocks, KNOT * 8), jnp.float32), jnp.zeros((2, NCAL), jnp.float32))
    (partial_value, calib_terms), _ = lax.scan(accumulate, start, inputs)
    outgoing = partial_value.reshape(devices, LIST, KNOT * 8)
    arrived = lax.all_to_all(outgoing, ("src", "att"), split_axis=0, concat_axis=0, tiled=True)
    totals = lax.psum(calib_terms, ("src", "att"))
    calib_update = totals[0] / (totals[1] + 1.0)
    listed = time_list.reshape(devices * LIST)
    selector = (listed[None, :] == jnp.arange(KB_DEV, dtype=jnp.int32)[:, None]).astype(jnp.float32)
    owned = jnp.dot(
        selector,
        arrived.reshape(devices * LIST, KNOT * 8),
        precision=HIGH,
        preferred_element_type=jnp.float32,
    )
    owned = owned.reshape(KB_DEV, KNOT, 8)
    update = owned[:, :, 0:4] / (owned[:, :, 4:8] + 1.0)
    attitude_update = update.reshape(KB_DEV * KNOT, 4).T
    returning = jnp.dot(
        selector.T,
        update.reshape(KB_DEV, KNOT * 4),
        precision=HIGH,
        preferred_element_type=jnp.float32,
    )
    returning = returning.reshape(devices, LIST, KNOT * 4)
    segment = lax.all_to_all(returning, ("src", "att"), split_axis=0, concat_axis=0, tiled=True)
    segment_rows = segment.reshape(listed_blocks, KNOT * 4)

    def correct(carry, inputs):
        blocks, knot_first, basis_part, attitude_block, calib_ids_part, calib_coef, first_part = (
            inputs
        )
        selector_rows = (blocks[:, None] == block_ids).astype(jnp.float32)
        fetched = jnp.dot(
            selector_rows, segment_rows, precision=HIGH, preferred_element_type=jnp.float32
        )
        fetched = fetched.reshape(step_rows, KNOT, 4)
        projected = jnp.sum(fetched * attitude_block[:, None, :], axis=2)
        linear = knot_rows(basis_part, knot_first, False)
        attitude_term = jnp.sum(linear * projected, axis=1)
        calib_hot = (calib_ids_part[:, None] == calib_ids).astype(jnp.float32)
        calib_value = jnp.dot(
            calib_hot, calib_update, precision=HIGH, preferred_element_type=jnp.float32
        )
        return (carry, first_part - attitude_term - calib_coef * calib_value)

    inputs_back = (
        block_id.reshape(steps, step_rows),
        obs_knot.reshape(steps, step_rows),
        basis_rows.reshape(steps, step_rows, 4),
        attitude_rows.reshape(steps, step_rows, 4),
        obs_calib.reshape(steps, step_rows),
        calib_part.reshape(steps, step_rows),
        first.reshape(steps, step_rows),
    )
    _, residual_blocks = lax.scan(correct, jnp.float32(0.0), inputs_back)
    residual_out = residual_blocks.reshape(count)
    return (source_update, attitude_update, calib_update, residual_out)


def solution(mesh):
    placed = (
        P(("src", "att")),
        P(("src", "att")),
        P(None, ("src", "att")),
        P(None, ("src", "att")),
        P(("src", "att")),
        P(("src", "att")),
        P(("src", "att")),
        P(("src", "att")),
        P(("src", "att")),
        P(("src", "att")),
        P(("src", "att")),
        P(("src", "att"), None),
        P(None, ("src", "att"), None),
    )
    return jax.shard_map(
        on_device,
        mesh=mesh,
        in_specs=placed,
        out_specs=(P(None, ("src", "att")), P(None, ("src", "att")), P(), P(("src", "att"))),
        check_vma=False,
    )
```

profile of v0, /device:TPU:0, one launch (start us, length us, event | category | flops | bytes accessed | tf_op | source)
XLA Modules:
  0.0 256.5 jit_solution(3903458531358402341)
XLA Ops:
  11.1 87.2 %while.25 = (s32[]{:T(128)}, f32[128,1024]{1,0:T(8,128)S(1)}, f32[2,2048]{1,0:T(2,128)S(1)}, s32[4,2048]{1,0:T(4,128)S(1)}, s32[4,2048]{1,0:T(4,128)S(1)}, /*ind...) while((s32[]{:T(128)}, f32[128,1024]{1,0:T(8,128)S(1)}, ...), condition=%wide.region_2.3_spmd.clone, body=%wide.region_1.2_spmd.clone.sunk | while | flops 3335804928 | bytes 22626460 | solution.py:159
  18.4 9.3 %fusion.136 = f32[128,1024]{1,0:T(8,128)S(1)} fusion(f32[2048,128,4]{0,2,1:T(4,128)} %broadcast_multiply_fusion.4, f32[2048,128,4]{0,2,1:T(4,128)} %broadcast_multiply_fusion.5, f32[128,1024]{1,0:T(8,128)S(1)} %get-tuple-element.580, s32[2048]{0:T(1024)S(1)} %bitcast.454, pred[]{:T(512)S(6)} %compare.4), kind=kOutput, calls=%fused_computation.37.clone.1 | convolution fusion | flops 3224109056 | bytes 9445377 | tf_op jit(solution)/shard_map/while/body/eval_jaxpr/ib,im->bm/dot_general | solution.py:140
  27.7 5.4 %fusion.137 = f32[2,2048]{1,0:T(2,128)S(1)} fusion(s32[2048]{0:T(1024)S(1)} %bitcast.470, f32[2,2048]{1,0:T(2,128)S(1)} %get-tuple-element.581, f32[4,2048,2]{1,2,0:T(2,128)S(1)} %get-tuple-element.599, s32[]{:T(128)S(6)} %copy.66, pred[]{:T(512)S(6)} %compare.4), kind=kOutput, calls=%fused_computation.34.clone.1 | convolution fusion | flops 104865792 | bytes 57349 | tf_op jit(solution)/shard_map/while/body/eval_jaxpr/in,ic->cn/dot_general | solution.py:144
  40.1 9.3 %fusion.136 = f32[128,1024]{1,0:T(8,128)S(1)} fusion(f32[2048,128,4]{0,2,1:T(4,128)} %broadcast_multiply_fusion.4, f32[2048,128,4]{0,2,1:T(4,128)} %broadcast_multiply_fusion.5, f32[128,1024]{1,0:T(8,128)S(1)} %get-tuple-element.580, s32[2048]{0:T(1024)S(1)} %bitcast.454, pred[]{:T(512)S(6)} %compare.4), kind=kOutput, calls=%fused_computation.37.clone.1 | convolution fusion | flops 3224109056 | bytes 9445377 | tf_op jit(solution)/shard_map/while/body/eval_jaxpr/ib,im->bm/dot_general | solution.py:140
  49.4 5.4 %fusion.137 = f32[2,2048]{1,0:T(2,128)S(1)} fusion(s32[2048]{0:T(1024)S(1)} %bitcast.470, f32[2,2048]{1,0:T(2,128)S(1)} %get-tuple-element.581, f32[4,2048,2]{1,2,0:T(2,128)S(1)} %get-tuple-element.599, s32[]{:T(128)S(6)} %copy.66, pred[]{:T(512)S(6)} %compare.4), kind=kOutput, calls=%fused_computation.34.clone.1 | convolution fusion | flops 104865792 | bytes 57349 | tf_op jit(solution)/shard_map/while/body/eval_jaxpr/in,ic->cn/dot_general | solution.py:144
  61.8 9.3 %fusion.136 = f32[128,1024]{1,0:T(8,128)S(1)} fusion(f32[2048,128,4]{0,2,1:T(4,128)} %broadcast_multiply_fusion.4, f32[2048,128,4]{0,2,1:T(4,128)} %broadcast_multiply_fusion.5, f32[128,1024]{1,0:T(8,128)S(1)} %get-tuple-element.580, s32[2048]{0:T(1024)S(1)} %bitcast.454, pred[]{:T(512)S(6)} %compare.4), kind=kOutput, calls=%fused_computation.37.clone.1 | convolution fusion | flops 3224109056 | bytes 9445377 | tf_op jit(solution)/shard_map/while/body/eval_jaxpr/ib,im->bm/dot_general | solution.py:140
  71.1 5.4 %fusion.137 = f32[2,2048]{1,0:T(2,128)S(1)} fusion(s32[2048]{0:T(1024)S(1)} %bitcast.470, f32[2,2048]{1,0:T(2,128)S(1)} %get-tuple-element.581, f32[4,2048,2]{1,2,0:T(2,128)S(1)} %get-tuple-element.599, s32[]{:T(128)S(6)} %copy.66, pred[]{:T(512)S(6)} %compare.4), kind=kOutput, calls=%fused_computation.34.clone.1 | convolution fusion | flops 104865792 | bytes 57349 | tf_op jit(solution)/shard_map/while/body/eval_jaxpr/in,ic->cn/dot_general | solution.py:144
  83.5 9.3 %fusion.136 = f32[128,1024]{1,0:T(8,128)S(1)} fusion(f32[2048,128,4]{0,2,1:T(4,128)} %broadcast_multiply_fusion.4, f32[2048,128,4]{0,2,1:T(4,128)} %broadcast_multiply_fusion.5, f32[128,1024]{1,0:T(8,128)S(1)} %get-tuple-element.580, s32[2048]{0:T(1024)S(1)} %bitcast.454, pred[]{:T(512)S(6)} %compare.4), kind=kOutput, calls=%fused_computation.37.clone.1 | convolution fusion | flops 3224109056 | bytes 9445377 | tf_op jit(solution)/shard_map/while/body/eval_jaxpr/ib,im->bm/dot_general | solution.py:140
  92.8 5.4 %fusion.137 = f32[2,2048]{1,0:T(2,128)S(1)} fusion(s32[2048]{0:T(1024)S(1)} %bitcast.470, f32[2,2048]{1,0:T(2,128)S(1)} %get-tuple-element.581, f32[4,2048,2]{1,2,0:T(2,128)S(1)} %get-tuple-element.599, s32[]{:T(128)S(6)} %copy.66, pred[]{:T(512)S(6)} %compare.4), kind=kOutput, calls=%fused_computation.34.clone.1 | convolution fusion | flops 104865792 | bytes 57349 | tf_op jit(solution)/shard_map/while/body/eval_jaxpr/in,ic->cn/dot_general | solution.py:144
  99.3 7.3 %all-to-all-start = ((f32[32,4,1024]{2,1,0:T(4,128)}), f32[32,4,1024]{2,1,0:T(4,128)S(1)}, u32[]{:S(2)}, u32[]{:S(2)}) async-start(f32[32,4,1024]{2,1,0:T(4,128)} %reshape.3148), calls=%async_computation | async-start | bytes 1048576 | tf_op jit(solution)/shard_map/all_to_all | solution.py:161
  107.6 40.8 %psum.7 = f32[2,2048]{1,0:T(2,128)S(1)} all-reduce(f32[2,2048]{1,0:T(2,128)S(1)} %get-tuple-element.135), channel_id=1, replica_groups=mesh['src'=8,'att'=4] {'src','att'}, use_global_device_ids=true, to_apply=%region_3.4 | all-reduce | flops 4096 | bytes 32768 | tf_op jit(solution)/shard_map/psum | solution.py:162
  155.6 9.9 %all-to-all-done.1 = f32[32,4,512]{2,1,0:T(4,128)S(1)} async-done(((f32[32,4,512]{2,1,0:T(4,128)}), f32[32,4,512]{2,1,0:T(4,128)S(1)}, u32[]{:S(2)}, u32[]{:S(2)}) %all-to-all-start.1) | async-done | bytes 262176 | tf_op jit(solution)/shard_map/all_to_all | solution.py:182
  165.7 90.2 %while.24 = (s32[]{:T(128)}, f32[4,2048]{1,0:T(4,128)S(1)}, f32[4,2048]{1,0:T(4,128)S(1)}, s32[4,2048]{1,0:T(4,128)S(1)}, f32[4,2048,4]{1,2,0:T(4,128)S(1)}, /*i...) while((s32[]{:T(128)}, f32[4,2048]{1,0:T(4,128)S(1)}, ...), condition=%wide.region_7.8_spmd.clone, body=%wide.region_4.7_spmd.clone.sunk | while | flops 1670653952 | bytes 19644568 | solution.py:212
  165.7 7.5 %fusion.130 = f32[1,2048]{1,0:T(1,128)S(1)} fusion(f32[2048,1]{0,1:T(1,128)S(1)} %bitcast.504, s32[2048]{0:T(1024)S(1)} %bitcast.471), kind=kOutput, calls=%fused_computation.5.clone.1 | convolution fusion | flops 54525952 | bytes 24576 | tf_op jit(solution)/shard_map/while/body/eval_jaxpr/dot_general | solution.py:198
  177.0 5.2 %reshape.3266 = f32[2048,128,4]{0,2,1:T(4,128)} reshape(f32[2048,512]{0,1:T(8,128)} %fusion.131) | data formatting | bytes 8388608 | tf_op jit(solution)/shard_map/while/body/eval_jaxpr/reshape | solution.py:193
  182.2 5.3 %multiply_reduce_fusion.5 = f32[2048,128]{0,1:T(8,128)S(1)} fusion(f32[2048,128,4]{0,2,1:T(4,128)} %reshape.3266, f32[2048,4]{0,1:T(4,128)S(1)} %get-tuple-element.531), kind=kLoop, calls=%fused_computation.7.clone.1 | loop fusion | flops 1835008 | bytes 5275648 | tf_op jit(solution)/shard_map/while/body/eval_jaxpr/reduce_sum | solution.py:194
  188.3 7.5 %fusion.130 = f32[1,2048]{1,0:T(1,128)S(1)} fusion(f32[2048,1]{0,1:T(1,128)S(1)} %bitcast.504, s32[2048]{0:T(1024)S(1)} %bitcast.471), kind=kOutput, calls=%fused_computation.5.clone.1 | convolution fusion | flops 54525952 | bytes 24576 | tf_op jit(solution)/shard_map/while/body/eval_jaxpr/dot_general | solution.py:198
  199.6 5.2 %reshape.3266 = f32[2048,128,4]{0,2,1:T(4,128)} reshape(f32[2048,512]{0,1:T(8,128)} %fusion.131) | data formatting | bytes 8388608 | tf_op jit(solution)/shard_map/while/body/eval_jaxpr/reshape | solution.py:193
  204.7 5.3 %multiply_reduce_fusion.5 = f32[2048,128]{0,1:T(8,128)S(1)} fusion(f32[2048,128,4]{0,2,1:T(4,128)} %reshape.3266, f32[2048,4]{0,1:T(4,128)S(1)} %get-tuple-element.531), kind=kLoop, calls=%fused_computation.7.clone.1 | loop fusion | flops 1835008 | bytes 5275648 | tf_op jit(solution)/shard_map/while/body/eval_jaxpr/reduce_sum | solution.py:194
  210.8 7.5 %fusion.130 = f32[1,2048]{1,0:T(1,128)S(1)} fusion(f32[2048,1]{0,1:T(1,128)S(1)} %bitcast.504, s32[2048]{0:T(1024)S(1)} %bitcast.471), kind=kOutput, calls=%fused_computation.5.clone.1 | convolution fusion | flops 54525952 | bytes 24576 | tf_op jit(solution)/shard_map/while/body/eval_jaxpr/dot_general | solution.py:198
  222.1 5.2 %reshape.3266 = f32[2048,128,4]{0,2,1:T(4,128)} reshape(f32[2048,512]{0,1:T(8,128)} %fusion.131) | data formatting | bytes 8388608 | tf_op jit(solution)/shard_map/while/body/eval_jaxpr/reshape | solution.py:193
  227.3 5.3 %multiply_reduce_fusion.5 = f32[2048,128]{0,1:T(8,128)S(1)} fusion(f32[2048,128,4]{0,2,1:T(4,128)} %reshape.3266, f32[2048,4]{0,1:T(4,128)S(1)} %get-tuple-element.531), kind=kLoop, calls=%fused_computation.7.clone.1 | loop fusion | flops 1835008 | bytes 5275648 | tf_op jit(solution)/shard_map/while/body/eval_jaxpr/reduce_sum | solution.py:194
  233.4 7.5 %fusion.130 = f32[1,2048]{1,0:T(1,128)S(1)} fusion(f32[2048,1]{0,1:T(1,128)S(1)} %bitcast.504, s32[2048]{0:T(1024)S(1)} %bitcast.471), kind=kOutput, calls=%fused_computation.5.clone.1 | convolution fusion | flops 54525952 | bytes 24576 | tf_op jit(solution)/shard_map/while/body/eval_jaxpr/dot_general | solution.py:198
  249.8 5.3 %multiply_reduce_fusion.5 = f32[2048,128]{0,1:T(8,128)S(1)} fusion(f32[2048,128,4]{0,2,1:T(4,128)} %reshape.3266, f32[2048,4]{0,1:T(4,128)S(1)} %get-tuple-element.531), kind=kLoop, calls=%fused_computation.7.clone.1 | loop fusion | flops 1835008 | bytes 5275648 | tf_op jit(solution)/shard_map/while/body/eval_jaxpr/reduce_sum | solution.py:194
  (178 shorter events, 70.9 us)
Async XLA Ops:
  0.6 0.7 copy-start
  0.6 10.0 %copy-start.1 = (f32[5,8192]{1,0:T(8,128)S(1)}, f32[5,8192]{1,0:T(8,128)}, u32[]{:S(2)}) copy-start(f32[5,8192]{1,0:T(8,128)} %param.19) | copy-start | bytes 491524
  0.7 10.1 %copy-start.3 = (f32[8192]{0:T(1024)S(1)}, f32[8192]{0:T(1024)}, u32[]{:S(2)}) copy-start(f32[8192]{0:T(1024)} %param.21) | copy-start | bytes 98308
  0.7 10.1 %copy-start.4 = (f32[8192]{0:T(1024)S(1)}, f32[8192]{0:T(1024)}, u32[]{:S(2)}) copy-start(f32[8192]{0:T(1024)} %param.17) | copy-start | bytes 98308
  0.7 7.3 %copy-start.5 = (s32[8192]{0:T(1024)S(1)}, s32[8192]{0:T(1024)}, u32[]{:S(2)}) copy-start(s32[8192]{0:T(1024)} %param.25) | copy-start | bytes 98308
  0.7 7.3 %copy-start.6 = (s32[8192]{0:T(1024)S(1)}, s32[8192]{0:T(1024)}, u32[]{:S(2)}) copy-start(s32[8192]{0:T(1024)} %param.24) | copy-start | bytes 98308
  0.7 7.4 %copy-start.8 = (s32[8192]{0:T(1024)S(1)}, s32[8192]{0:T(1024)}, u32[]{:S(2)}) copy-start(s32[8192]{0:T(1024)} %param.26) | copy-start | bytes 98308
  0.7 7.4 %copy-start.7 = (f32[8192]{0:T(1024)S(1)}, f32[8192]{0:T(1024)}, u32[]{:S(2)}) copy-start(f32[8192]{0:T(1024)} %param.22) | copy-start | bytes 98308
  0.7 10.1 %copy-start.9 = (s32[8192]{0:T(1024)S(1)}, s32[8192]{0:T(1024)}, u32[]{:S(2)}) copy-start(s32[8192]{0:T(1024)} %param.27) | copy-start | bytes 98308
  0.7 10.1 %copy-start.2 = (f32[4,8192]{1,0:T(4,128)S(1)}, f32[4,8192]{1,0:T(4,128)}, u32[]{:S(2)}) copy-start(f32[4,8192]{1,0:T(4,128)} %param.20) | copy-start | bytes 393220
  11.1 95.5 %copy-start.10 = (s32[32,1,4]{0,2,1:T(4,128)S(1)}, s32[32,1,4]{0,2,1:T(4,128)}, u32[]{:S(2)}) copy-start(s32[32,1,4]{0,2,1:T(4,128)} %param.29) | copy-start | bytes 1540
  99.3 49.1 %all-to-all-start = ((f32[32,4,1024]{2,1,0:T(4,128)}), f32[32,4,1024]{2,1,0:T(4,128)S(1)}, u32[]{:S(2)}, u32[]{:S(2)}) async-start(f32[32,4,1024]{2,1,0:T(4,128)} %reshape.3148), calls=%async_computation | async-start | bytes 1048576 | tf_op jit(solution)/shard_map/all_to_all | solution.py:161
  150.5 15.0 %all-to-all-start.1 = ((f32[32,4,512]{2,1,0:T(4,128)}), f32[32,4,512]{2,1,0:T(4,128)S(1)}, u32[]{:S(2)}, u32[]{:S(2)}) async-start(f32[32,4,512]{2,1,0:T(4,128)} %copy.46), calls=%async_computation.1 | async-start | bytes 524288 | tf_op jit(solution)/shard_map/all_to_all | solution.py:182
  255.9 0.6 copy-start.11
where the time goes:
time: 258 us; the launch traced here: 256 us
  matrix products  106 us (41%)
  other arithmetic  53.4 us (21%)
  blocking collectives  40.8 us (16%)
  local copies, waits for them, and re-layouts  32.3 us (13%)
  starting transfers between devices  11.7 us (5%)
  waiting for transfers between devices  9.94 us (4%)
    psum x1, blocking collectives, on_device(): totals = lax.psum(calib_terms, ('src', 'att'))  40.8 us
    dot_general x4, matrix products, accumulate(): jnp.einsum('ib,im->bm', selector, spread, precision=HIGH, preferred_eleme...  37.2 us
    dot_general x4, matrix products, correct(): jnp.dot(calib_hot, calib_update, precision=HIGH, preferred_element_type=j...  30.1 us
    dot_general x4, matrix products, accumulate(): jnp.einsum('in,ic->cn', calib_hot, calib_vals, precision=HIGH, preferred_...  21.4 us
    reduce_sum x4, other arithmetic, correct(): projected = jnp.sum(fetched * attitude_block[:, None, :], axis=2)  21.3 us
    reshape x4, local copies, waits for them, and re-layouts, correct(): fetched = fetched.reshape(step_rows, KNOT, 4)  20.7 us
    dot_general x4, matrix products, correct(): jnp.dot(selector_rows, segment_rows, precision=HIGH, preferred_element_ty...  15 us
    mul x4, other arithmetic, accumulate(): linear[:, :, None] * rhs_part[:, None, :]  12.7 us
  transfers between devices with their start and end apart: 2, of which 1 were waited for; matrix products, arithmetic and copies ran while one was open for 1% of the time, Pallas kernels for 0%

commit v1 on v0

--- a/solution.py
+++ b/solution.py
@@ -159,7 +159,8 @@
     (partial_value, calib_terms), _ = lax.scan(accumulate, start, inputs)
     outgoing = partial_value.reshape(devices, LIST, KNOT * 8)
     arrived = lax.all_to_all(outgoing, ("src", "att"), split_axis=0, concat_axis=0, tiled=True)
-    totals = lax.psum(calib_terms, ("src", "att"))
+    parts = lax.all_gather(calib_terms, ("src", "att"))
+    totals = jnp.sum(parts, axis=0)
     calib_update = totals[0] / (totals[1] + 1.0)
     listed = time_list.reshape(devices * LIST)
     selector = (listed[None, :] == jnp.arange(KB_DEV, dtype=jnp.int32)[:, None]).astype(jnp.float32)

time: 258 us -> 260 us (level)
  blocking collectives: 40.8 us -> 45.2 us
    all_gather x0 -> x1, blocking collectives: none -> 45.2 us  [on_device(): parts = lax.all_gather(calib_terms, ('src', 'att'))]
    psum x1 -> x0, blocking collectives: 40.8 us -> none  [on_device(): totals = lax.psum(calib_terms, ('src', 'att'))]
where the time goes in v1:
time: 260 us; the launch traced here: 259 us
  matrix products  106 us (41%)
  other arithmetic  53.6 us (21%)
  blocking collectives  45.2 us (17%)
  local copies, waits for them, and re-layouts  32.3 us (12%)
  waiting for transfers between devices  9.94 us (4%)
  starting transfers between devices  9.88 us (4%)
    all_gather x1, blocking collectives, on_device(): parts = lax.all_gather(calib_terms, ('src', 'att'))  45.2 us
    dot_general x4, matrix products, accumulate(): jnp.einsum('ib,im->bm', selector, spread, precision=HIGH, preferred_eleme...  37.2 us
    dot_general x4, matrix products, correct(): jnp.dot(calib_hot, calib_update, precision=HIGH, preferred_element_type=j...  30.1 us
    dot_general x4, matrix products, accumulate(): jnp.einsum('in,ic->cn', calib_hot, calib_vals, precision=HIGH, preferred_...  21.4 us
    reduce_sum x4, other arithmetic, correct(): projected = jnp.sum(fetched * attitude_block[:, None, :], axis=2)  21.3 us
    reshape x4, local copies, waits for them, and re-layouts, correct(): fetched = fetched.reshape(step_rows, KNOT, 4)  20.7 us
    dot_general x4, matrix products, correct(): jnp.dot(selector_rows, segment_rows, precision=HIGH, preferred_element_ty...  15 us
    mul x4, other arithmetic, accumulate(): linear[:, :, None] * rhs_part[:, None, :]  12.7 us
  transfers between devices with their start and end apart: 2, of which 1 were waited for; matrix products, arithmetic and copies ran while one was open for 1% of the time, Pallas kernels for 0%

profile of v1, /device:TPU:0, one launch (start us, length us, event | category | flops | bytes accessed | tf_op | source)
XLA Modules:
  0.0 259.1 jit_solution(3131968893809487225)
XLA Ops:
  11.1 87.2 %while.25 = (s32[]{:T(128)}, f32[128,1024]{1,0:T(8,128)S(1)}, f32[2,2048]{1,0:T(2,128)S(1)}, s32[4,2048]{1,0:T(4,128)S(1)}, s32[4,2048]{1,0:T(4,128)S(1)}, /*ind...) while((s32[]{:T(128)}, f32[128,1024]{1,0:T(8,128)S(1)}, ...), condition=%wide.region_2.3_spmd.clone, body=%wide.region_1.2_spmd.clone.sunk | while | flops 3335804928 | bytes 22626460 | solution.py:159
  18.4 9.3 %fusion.136 = f32[128,1024]{1,0:T(8,128)S(1)} fusion(f32[2048,128,4]{0,2,1:T(4,128)} %broadcast_multiply_fusion.4, f32[2048,128,4]{0,2,1:T(4,128)} %broadcast_multiply_fusion.5, f32[128,1024]{1,0:T(8,128)S(1)} %get-tuple-element.580, s32[2048]{0:T(1024)S(1)} %bitcast.455, pred[]{:T(512)S(6)} %compare.4), kind=kOutput, calls=%fused_computation.37.clone.1 | convolution fusion | flops 3224109056 | bytes 9445377 | tf_op jit(solution)/shard_map/while/body/eval_jaxpr/ib,im->bm/dot_general | solution.py:140
  27.7 5.4 %fusion.137 = f32[2,2048]{1,0:T(2,128)S(1)} fusion(s32[2048]{0:T(1024)S(1)} %bitcast.471, f32[2,2048]{1,0:T(2,128)S(1)} %get-tuple-element.581, f32[4,2048,2]{1,2,0:T(2,128)S(1)} %get-tuple-element.599, s32[]{:T(128)S(6)} %copy.66, pred[]{:T(512)S(6)} %compare.4), kind=kOutput, calls=%fused_computation.34.clone.1 | convolution fusion | flops 104865792 | bytes 57349 | tf_op jit(solution)/shard_map/while/body/eval_jaxpr/in,ic->cn/dot_general | solution.py:144
  40.1 9.3 %fusion.136 = f32[128,1024]{1,0:T(8,128)S(1)} fusion(f32[2048,128,4]{0,2,1:T(4,128)} %broadcast_multiply_fusion.4, f32[2048,128,4]{0,2,1:T(4,128)} %broadcast_multiply_fusion.5, f32[128,1024]{1,0:T(8,128)S(1)} %get-tuple-element.580, s32[2048]{0:T(1024)S(1)} %bitcast.455, pred[]{:T(512)S(6)} %compare.4), kind=kOutput, calls=%fused_computation.37.clone.1 | convolution fusion | flops 3224109056 | bytes 9445377 | tf_op jit(solution)/shard_map/while/body/eval_jaxpr/ib,im->bm/dot_general | solution.py:140
  49.4 5.4 %fusion.137 = f32[2,2048]{1,0:T(2,128)S(1)} fusion(s32[2048]{0:T(1024)S(1)} %bitcast.471, f32[2,2048]{1,0:T(2,128)S(1)} %get-tuple-element.581, f32[4,2048,2]{1,2,0:T(2,128)S(1)} %get-tuple-element.599, s32[]{:T(128)S(6)} %copy.66, pred[]{:T(512)S(6)} %compare.4), kind=kOutput, calls=%fused_computation.34.clone.1 | convolution fusion | flops 104865792 | bytes 57349 | tf_op jit(solution)/shard_map/while/body/eval_jaxpr/in,ic->cn/dot_general | solution.py:144
  61.8 9.3 %fusion.136 = f32[128,1024]{1,0:T(8,128)S(1)} fusion(f32[2048,128,4]{0,2,1:T(4,128)} %broadcast_multiply_fusion.4, f32[2048,128,4]{0,2,1:T(4,128)} %broadcast_multiply_fusion.5, f32[128,1024]{1,0:T(8,128)S(1)} %get-tuple-element.580, s32[2048]{0:T(1024)S(1)} %bitcast.455, pred[]{:T(512)S(6)} %compare.4), kind=kOutput, calls=%fused_computation.37.clone.1 | convolution fusion | flops 3224109056 | bytes 9445377 | tf_op jit(solution)/shard_map/while/body/eval_jaxpr/ib,im->bm/dot_general | solution.py:140
  71.1 5.4 %fusion.137 = f32[2,2048]{1,0:T(2,128)S(1)} fusion(s32[2048]{0:T(1024)S(1)} %bitcast.471, f32[2,2048]{1,0:T(2,128)S(1)} %get-tuple-element.581, f32[4,2048,2]{1,2,0:T(2,128)S(1)} %get-tuple-element.599, s32[]{:T(128)S(6)} %copy.66, pred[]{:T(512)S(6)} %compare.4), kind=kOutput, calls=%fused_computation.34.clone.1 | convolution fusion | flops 104865792 | bytes 57349 | tf_op jit(solution)/shard_map/while/body/eval_jaxpr/in,ic->cn/dot_general | solution.py:144
  83.5 9.3 %fusion.136 = f32[128,1024]{1,0:T(8,128)S(1)} fusion(f32[2048,128,4]{0,2,1:T(4,128)} %broadcast_multiply_fusion.4, f32[2048,128,4]{0,2,1:T(4,128)} %broadcast_multiply_fusion.5, f32[128,1024]{1,0:T(8,128)S(1)} %get-tuple-element.580, s32[2048]{0:T(1024)S(1)} %bitcast.455, pred[]{:T(512)S(6)} %compare.4), kind=kOutput, calls=%fused_computation.37.clone.1 | convolution fusion | flops 3224109056 | bytes 9445377 | tf_op jit(solution)/shard_map/while/body/eval_jaxpr/ib,im->bm/dot_general | solution.py:140
  92.8 5.4 %fusion.137 = f32[2,2048]{1,0:T(2,128)S(1)} fusion(s32[2048]{0:T(1024)S(1)} %bitcast.471, f32[2,2048]{1,0:T(2,128)S(1)} %get-tuple-element.581, f32[4,2048,2]{1,2,0:T(2,128)S(1)} %get-tuple-element.599, s32[]{:T(128)S(6)} %copy.66, pred[]{:T(512)S(6)} %compare.4), kind=kOutput, calls=%fused_computation.34.clone.1 | convolution fusion | flops 104865792 | bytes 57349 | tf_op jit(solution)/shard_map/while/body/eval_jaxpr/in,ic->cn/dot_general | solution.py:144
  99.3 7.3 %all-to-all-start = ((f32[32,4,1024]{2,1,0:T(4,128)}), f32[32,4,1024]{2,1,0:T(4,128)S(1)}, u32[]{:S(2)}, u32[]{:S(2)}) async-start(f32[32,4,1024]{2,1,0:T(4,128)} %reshape.3148), calls=%async_computation | async-start | bytes 1048576 | tf_op jit(solution)/shard_map/all_to_all | solution.py:161
  106.8 45.2 %all-gather.1 = f32[32,2,2048]{2,1,0:T(2,128)S(1)} all-gather(f32[1,2,2048]{2,1,0:T(2,128)S(1)} %bitcast.502), channel_id=2, replica_groups=mesh['src'=8,'att'=4] {'src','att'}, dimensions={0}, use_global_device_ids=true | all-gather | bytes 540672 | tf_op jit(solution)/shard_map/all_gather | solution.py:162
  158.3 9.9 %all-to-all-done.1 = f32[32,4,512]{2,1,0:T(4,128)S(1)} async-done(((f32[32,4,512]{2,1,0:T(4,128)}), f32[32,4,512]{2,1,0:T(4,128)S(1)}, u32[]{:S(2)}, u32[]{:S(2)}) %all-to-all-start.1) | async-done | bytes 262176 | tf_op jit(solution)/shard_map/all_to_all | solution.py:183
  168.3 90.2 %while.24 = (s32[]{:T(128)}, f32[4,2048]{1,0:T(4,128)S(1)}, f32[4,2048]{1,0:T(4,128)S(1)}, s32[4,2048]{1,0:T(4,128)S(1)}, f32[4,2048,4]{1,2,0:T(4,128)S(1)}, /*i...) while((s32[]{:T(128)}, f32[4,2048]{1,0:T(4,128)S(1)}, ...), condition=%wide.region_7.8_spmd.clone, body=%wide.region_4.7_spmd.clone.sunk | while | flops 1670653952 | bytes 19644568 | solution.py:213
  168.4 7.5 %fusion.130 = f32[1,2048]{1,0:T(1,128)S(1)} fusion(f32[2048,1]{0,1:T(1,128)S(1)} %bitcast.506, s32[2048]{0:T(1024)S(1)} %bitcast.472), kind=kOutput, calls=%fused_computation.5.clone.1 | convolution fusion | flops 54525952 | bytes 24576 | tf_op jit(solution)/shard_map/while/body/eval_jaxpr/dot_general | solution.py:199
  179.7 5.2 %reshape.3270 = f32[2048,128,4]{0,2,1:T(4,128)} reshape(f32[2048,512]{0,1:T(8,128)} %fusion.131) | data formatting | bytes 8388608 | tf_op jit(solution)/shard_map/while/body/eval_jaxpr/reshape | solution.py:194
  184.8 5.3 %multiply_reduce_fusion.5 = f32[2048,128]{0,1:T(8,128)S(1)} fusion(f32[2048,128,4]{0,2,1:T(4,128)} %reshape.3270, f32[2048,4]{0,1:T(4,128)S(1)} %get-tuple-element.531), kind=kLoop, calls=%fused_computation.7.clone.1 | loop fusion | flops 1835008 | bytes 5275648 | tf_op jit(solution)/shard_map/while/body/eval_jaxpr/reduce_sum | solution.py:195
  190.9 7.5 %fusion.130 = f32[1,2048]{1,0:T(1,128)S(1)} fusion(f32[2048,1]{0,1:T(1,128)S(1)} %bitcast.506, s32[2048]{0:T(1024)S(1)} %bitcast.472), kind=kOutput, calls=%fused_computation.5.clone.1 | convolution fusion | flops 54525952 | bytes 24576 | tf_op jit(solution)/shard_map/while/body/eval_jaxpr/dot_general | solution.py:199
  202.2 5.2 %reshape.3270 = f32[2048,128,4]{0,2,1:T(4,128)} reshape(f32[2048,512]{0,1:T(8,128)} %fusion.131) | data formatting | bytes 8388608 | tf_op jit(solution)/shard_map/while/body/eval_jaxpr/reshape | solution.py:194
  207.4 5.3 %multiply_reduce_fusion.5 = f32[2048,128]{0,1:T(8,128)S(1)} fusion(f32[2048,128,4]{0,2,1:T(4,128)} %reshape.3270, f32[2048,4]{0,1:T(4,128)S(1)} %get-tuple-element.531), kind=kLoop, calls=%fused_computation.7.clone.1 | loop fusion | flops 1835008 | bytes 5275648 | tf_op jit(solution)/shard_map/while/body/eval_jaxpr/reduce_sum | solution.py:195
  213.5 7.5 %fusion.130 = f32[1,2048]{1,0:T(1,128)S(1)} fusion(f32[2048,1]{0,1:T(1,128)S(1)} %bitcast.506, s32[2048]{0:T(1024)S(1)} %bitcast.472), kind=kOutput, calls=%fused_computation.5.clone.1 | convolution fusion | flops 54525952 | bytes 24576 | tf_op jit(solution)/shard_map/while/body/eval_jaxpr/dot_general | solution.py:199
  224.7 5.2 %reshape.3270 = f32[2048,128,4]{0,2,1:T(4,128)} reshape(f32[2048,512]{0,1:T(8,128)} %fusion.131) | data formatting | bytes 8388608 | tf_op jit(solution)/shard_map/while/body/eval_jaxpr/reshape | solution.py:194
  229.9 5.3 %multiply_reduce_fusion.5 = f32[2048,128]{0,1:T(8,128)S(1)} fusion(f32[2048,128,4]{0,2,1:T(4,128)} %reshape.3270, f32[2048,4]{0,1:T(4,128)S(1)} %get-tuple-element.531), kind=kLoop, calls=%fused_computation.7.clone.1 | loop fusion | flops 1835008 | bytes 5275648 | tf_op jit(solution)/shard_map/while/body/eval_jaxpr/reduce_sum | solution.py:195
  236.0 7.5 %fusion.130 = f32[1,2048]{1,0:T(1,128)S(1)} fusion(f32[2048,1]{0,1:T(1,128)S(1)} %bitcast.506, s32[2048]{0:T(1024)S(1)} %bitcast.472), kind=kOutput, calls=%fused_computation.5.clone.1 | convolution fusion | flops 54525952 | bytes 24576 | tf_op jit(solution)/shard_map/while/body/eval_jaxpr/dot_general | solution.py:199
  252.4 5.3 %multiply_reduce_fusion.5 = f32[2048,128]{0,1:T(8,128)S(1)} fusion(f32[2048,128,4]{0,2,1:T(4,128)} %reshape.3270, f32[2048,4]{0,1:T(4,128)S(1)} %get-tuple-element.531), kind=kLoop, calls=%fused_computation.7.clone.1 | loop fusion | flops 1835008 | bytes 5275648 | tf_op jit(solution)/shard_map/while/body/eval_jaxpr/reduce_sum | solution.py:195
  (179 shorter events, 69.2 us)
Async XLA Ops:
  0.6 0.7 copy-start
  0.6 10.0 %copy-start.1 = (f32[5,8192]{1,0:T(8,128)S(1)}, f32[5,8192]{1,0:T(8,128)}, u32[]{:S(2)}) copy-start(f32[5,8192]{1,0:T(8,128)} %param.19) | copy-start | bytes 491524
  0.7 10.1 %copy-start.3 = (f32[8192]{0:T(1024)S(1)}, f32[8192]{0:T(1024)}, u32[]{:S(2)}) copy-start(f32[8192]{0:T(1024)} %param.21) | copy-start | bytes 98308
  0.7 10.1 %copy-start.4 = (f32[8192]{0:T(1024)S(1)}, f32[8192]{0:T(1024)}, u32[]{:S(2)}) copy-start(f32[8192]{0:T(1024)} %param.17) | copy-start | bytes 98308
  0.7 7.3 %copy-start.5 = (s32[8192]{0:T(1024)S(1)}, s32[8192]{0:T(1024)}, u32[]{:S(2)}) copy-start(s32[8192]{0:T(1024)} %param.25) | copy-start | bytes 98308
  0.7 7.3 %copy-start.6 = (s32[8192]{0:T(1024)S(1)}, s32[8192]{0:T(1024)}, u32[]{:S(2)}) copy-start(s32[8192]{0:T(1024)} %param.24) | copy-start | bytes 98308
  0.7 7.4 %copy-start.8 = (s32[8192]{0:T(1024)S(1)}, s32[8192]{0:T(1024)}, u32[]{:S(2)}) copy-start(s32[8192]{0:T(1024)} %param.26) | copy-start | bytes 98308
  0.7 7.4 %copy-start.7 = (f32[8192]{0:T(1024)S(1)}, f32[8192]{0:T(1024)}, u32[]{:S(2)}) copy-start(f32[8192]{0:T(1024)} %param.22) | copy-start | bytes 98308
  0.7 10.1 %copy-start.9 = (s32[8192]{0:T(1024)S(1)}, s32[8192]{0:T(1024)}, u32[]{:S(2)}) copy-start(s32[8192]{0:T(1024)} %param.27) | copy-start | bytes 98308
  0.7 10.1 %copy-start.2 = (f32[4,8192]{1,0:T(4,128)S(1)}, f32[4,8192]{1,0:T(4,128)}, u32[]{:S(2)}) copy-start(f32[4,8192]{1,0:T(4,128)} %param.20) | copy-start | bytes 393220
  11.1 95.5 %copy-start.10 = (s32[32,1,4]{0,2,1:T(4,128)S(1)}, s32[32,1,4]{0,2,1:T(4,128)}, u32[]{:S(2)}) copy-start(s32[32,1,4]{0,2,1:T(4,128)} %param.29) | copy-start | bytes 1540
  99.3 53.6 %all-to-all-start = ((f32[32,4,1024]{2,1,0:T(4,128)}), f32[32,4,1024]{2,1,0:T(4,128)S(1)}, u32[]{:S(2)}, u32[]{:S(2)}) async-start(f32[32,4,1024]{2,1,0:T(4,128)} %reshape.3148), calls=%async_computation | async-start | bytes 1048576 | tf_op jit(solution)/shard_map/all_to_all | solution.py:161
  155.0 13.2 %all-to-all-start.1 = ((f32[32,4,512]{2,1,0:T(4,128)}), f32[32,4,512]{2,1,0:T(4,128)S(1)}, u32[]{:S(2)}, u32[]{:S(2)}) async-start(f32[32,4,512]{2,1,0:T(4,128)} %copy.46), calls=%async_computation.1 | async-start | bytes 524288 | tf_op jit(solution)/shard_map/all_to_all | solution.py:183
  258.5 0.6 copy-start.11
